TPU v7x, 32 devices: a whole 2x2x4 slice. The times are simulated.
32 devices in a mesh: ep: 32 (over z, y, x, core).
Axes of the slice: x: 2, y: 2, z: 4, core: 2. Of those that a mesh axis runs over, the one named last changes fastest.
Arguments:
- tokens: bfloat16 [4096, 2048], P('ep'), may hold values from -6 to 6
- cotangent: bfloat16 [4096, 2048], P('ep'), may hold values from -1 to 1
- gates: float32 [4096, 8], P('ep'), may hold values from 0.1 to 1
- experts: int32 [4096, 8], P('ep'), may hold values from 0 to 31, all different within a row; in each aligned block of 128 rows (0 to 127, 128 to 255, ...) at most 48 rows name the same one
- owner: int32 [32], replicated, may hold values from 0 to 31, each once
- swapped: int32 [16], replicated, may hold values 0 or 1
- w_gate: bfloat16 [32, 2048, 768], P('ep'), may hold values from -0.125 to 0.125
- w_up: bfloat16 [32, 2048, 768], P('ep'), may hold values from -0.125 to 0.125
- w_down: bfloat16 [32, 768, 2048], P('ep'), may hold values from -0.21875 to 0.21875
Outputs:
- mixed: bfloat16 [4096, 2048], P('ep')
- in_grad: bfloat16 [4096, 2048], P('ep')
- gate_grad: float32 [4096, 8], P('ep')
Inputs may be any that keep to these rules, and one draw needn't show every extreme that they name: Each row names 8 different experts. In the rows of one device no expert is named by more than 48 rows, and in every draw some expert is named by exactly 48 rows of some device. `owner`: names each device index once.
All inputs are finite; a program needn't handle non-finite values.
Results may differ from a plain program's by a relative error of at most 0.0065.
Values may be sent and summed in bfloat16 or wider, within the bound.
A program may use at most 192 MiB of HBM per device.

v0:
```python
import jax
import jax.numpy as jnp
from jax import lax
from jax.sharding import PartitionSpec as P


def project_in(flat, wg, wu):
    act_a = jnp.dot(flat, wg, preferred_element_type=jnp.float32)
    act_b = jnp.dot(flat, wu, preferred_element_type=jnp.float32)
    return (act_a, act_b)


def project_out(act_a, act_b, wd):
    sig = jax.nn.sigmoid(act_a)
    hidden = (act_a * sig * act_b).astype(jnp.bfloat16)
    return jnp.dot(hidden, wd, preferred_element_type=jnp.float32).astype(jnp.bfloat16)


def project_back(cots, act_a, act_b, wg, wu, wd):
    sig = jax.nn.sigmoid(act_a)
    back_hidden = lax.dot_general(
        cots, wd, (((1,), (1,)), ((), ())), preferred_element_type=jnp.float32
    )
    grad_a = (back_hidden * act_b * sig * (1.0 + act_a * (1.0 - sig))).astype(jnp.bfloat16)
    grad_b = (back_hidden * act_a * sig).astype(jnp.bfloat16)
    pair_grad = lax.dot_general(
        grad_a, wg, (((1,), (1,)), ((), ())), preferred_element_type=jnp.float32
    )
    pair_grad = pair_grad + lax.dot_general(
        grad_b, wu, (((1,), (1,)), ((), ())), preferred_element_type=jnp.float32
    )
    return pair_grad.astype(jnp.bfloat16)


def body(tokens, cotangent, gates, experts, owner, swapped, w_gate, w_up, w_down):
    tok_rows, width = tokens.shape
    top_count = experts.shape[1]
    expert_total = owner.shape[0]
    hidden_width = w_gate.shape[2]
    count = lax.axis_size("ep")
    slots = tok_rows * top_count * 3 // (2 * expert_total)
    pairs = tok_rows * top_count
    devices = jnp.arange(count, dtype=jnp.int32)
    dev_flag = jnp.repeat(swapped, 2)
    step_dev = dev_flag * (1 - 2 * (devices % 2))
    holder = owner + jnp.sum(
        jnp.where(owner[:, None] == devices[None, :], step_dev[None, :], 0), axis=1
    )
    wg = w_gate[0]
    wu = w_up[0]
    wd = w_down[0]
    flat_e = experts.reshape(-1)
    chosen = flat_e[:, None] == jnp.arange(expert_total, dtype=jnp.int32)[None, :]
    target = jnp.sum(jnp.where(chosen, holder[None, :], 0), axis=1)
    hot = target[:, None] == devices[None, :]
    running = jnp.cumsum(hot.astype(jnp.int32), axis=0)
    rank = jnp.sum(jnp.where(hot, running, 0), axis=1) - 1
    place = target * slots + rank
    source = (
        jnp.full((count * slots,), pairs, jnp.int32)
        .at[place]
        .set(jnp.arange(pairs, dtype=jnp.int32))
    )
    row_of = source // top_count
    tok_pad = jnp.concatenate([tokens, jnp.zeros((1, width), jnp.bfloat16)], axis=0)
    cot_pad = jnp.concatenate([cotangent, jnp.zeros((1, width), jnp.bfloat16)], axis=0)
    gate_pad = jnp.concatenate([gates.reshape(-1), jnp.zeros((1,), jnp.float32)], axis=0)
    send_x = tok_pad[row_of].reshape(count, slots, width)
    send_c = (cot_pad[row_of].astype(jnp.float32) * gate_pad[source][:, None]).astype(jnp.bfloat16)
    send_c = send_c.reshape(count, slots, width)
    received = lax.all_to_all(send_x, "ep", split_axis=0, concat_axis=0, tiled=True)
    flat = received.reshape(-1, width)
    act_a, act_b = project_in(flat, wg, wu)
    out_rows = project_out(act_a, act_b, wd)
    back = lax.all_to_all(
        out_rows.reshape(received.shape), "ep", split_axis=0, concat_axis=0, tiled=True
    )
    returned = (
        back,
        act_a.reshape(received.shape[0], received.shape[1], hidden_width),
        act_b.reshape(received.shape[0], received.shape[1], hidden_width),
    )
    back = returned[0]
    cot_recv = lax.all_to_all(send_c, "ep", split_axis=0, concat_axis=0, tiled=True)
    act_a = returned[1].reshape(-1, hidden_width)
    act_b = returned[2].reshape(-1, hidden_width)
    pair_grad = project_back(cot_recv.reshape(-1, width), act_a, act_b, wg, wu, wd)
    grad_back = lax.all_to_all(
        pair_grad.reshape(cot_recv.shape), "ep", split_axis=0, concat_axis=0, tiled=True
    )
    out_pairs = (
        back.reshape(-1, width)[place].reshape(tok_rows, top_count, width).astype(jnp.float32)
    )
    grad_pairs = (
        grad_back.reshape(-1, width)[place].reshape(tok_rows, top_count, width).astype(jnp.float32)
    )
    mixed = jnp.sum(gates[:, :, None] * out_pairs, axis=1).astype(jnp.bfloat16)
    gate_grad = jnp.sum(cotangent.astype(jnp.float32)[:, None, :] * out_pairs, axis=2)
    in_grad = jnp.sum(grad_pairs, axis=1).astype(jnp.bfloat16)
    return (mixed, in_grad, gate_grad)


def solution(mesh):
    return jax.shard_map(
        body,
        mesh=mesh,
        in_specs=(
            P("ep", None),
            P("ep", None),
            P("ep", None),
            P("ep", None),
            P(),
            P(),
            P("ep", None, None),
            P("ep", None, None),
            P("ep", None, None),
        ),
        out_specs=(P("ep", None), P("ep", None), P("ep", None)),
        check_vma=False,
    )
```

profile of v0, /device:TPU:0, one launch (start us, length us, event | category | flops | bytes accessed | tf_op | source)
XLA Modules:
  0.0 630.8 jit_solution(8266817931136488877)
XLA Ops:
  0.6 0.9 broadcast_in_dim.35
  1.6 0.8 select_reduce_fusion.1
  2.5 0.7 add.73
  3.1 0.8 copy.25
  4.1 9.0 %reduce-window.6 = s32[32,8,128]{2,1,0:T(8,128)S(1)} reduce-window(s32[32,8,128]{2,1,0:T(8,128)S(1)} %fusion.18, s32[]{:T(128)} %constant.47.clone.1), window={size=1x1x128 pad=0_0x0_0x127_0}, to_apply=%region_2.3 | reduce-window | flops 4161536 | bytes 262148 | tf_op jit(solution)/shard_map/reduce-window
  13.7 4.3 scatter_custom_fusion
  18.0 1.9 concatenate.9
  19.9 13.8 %gather_fusion = bf16[1536,2048]{1,0:T(8,128)(2,1)} fusion(bf16[129,2048]{1,0:T(8,128)(2,1)} %concatenate.9, s32[2048]{0:T(1024)S(1)} %get-tuple-element.14), kind=kCustom, calls=%fused_computation | custom fusion | bytes 12589056 | tf_op jit(solution)/shard_map/gather | solution.py:68
  33.7 7.4 %all-to-all-start = ((bf16[32,48,2048]{2,1,0:T(8,128)(2,1)}), bf16[32,48,2048]{2,1,0:T(8,128)(2,1)}, u32[]{:S(2)}, u32[]{:S(2)}) async-start(bf16[32,48,2048]{2,1,0:T(8,128)(2,1)} %bitcast.51), calls=%async_computation | async-start | bytes 12582912 | tf_op jit(solution)/shard_map/all_to_all | solution.py:71
  41.4 8.4 %gather_fusion.3 = f32[1536]{0:T(1024)S(1)} fusion(f32[1025]{0:T(1024)S(1)} %pad_maximum_fusion, s32[2048]{0:T(1024)S(1)} %get-tuple-element.13), kind=kCustom, calls=%fused_computation.3 | custom fusion | bytes 18432 | tf_op jit(solution)/shard_map/gather | solution.py:69
  49.8 1.9 concatenate.10
  51.8 13.8 %gather_fusion.2 = bf16[1536,2048]{1,0:T(8,128)(2,1)} fusion(bf16[129,2048]{1,0:T(8,128)(2,1)} %concatenate.10, s32[2048]{0:T(1024)S(1)} %get-tuple-element.14), kind=kCustom, calls=%fused_computation.2 | custom fusion | bytes 12589056 | tf_op jit(solution)/shard_map/gather | solution.py:69
  65.6 6.5 %fusion = bf16[32,48,2048]{2,1,0:T(8,128)(2,1)} fusion(bf16[32,48,2048]{2,1,0:T(8,128)(2,1)} %bitcast.52, f32[32,48]{1,0:T(8,128)S(1)} %mul.92), kind=kLoop, calls=%fused_computation.7 | loop fusion | flops 9437184 | bytes 12589056 | tf_op jit(solution)/shard_map/convert_element_type | solution.py:69
  72.1 109.1 %all-to-all-done = bf16[32,48,2048]{2,1,0:T(8,128)(2,1)} async-done(((bf16[32,48,2048]{2,1,0:T(8,128)(2,1)}), bf16[32,48,2048]{2,1,0:T(8,128)(2,1)}, u32[]{:S(2)}, u32[]{:S(2)}) %all-to-all-start) | async-done | bytes 6291488 | tf_op jit(solution)/shard_map/all_to_all | solution.py:71
  181.2 3.8 all-to-all-start.2
  185.0 8.2 %fusion.11 = f32[1536,768]{1,0:T(8,128)S(1)} fusion(bf16[1536,2048]{1,0:T(8,128)(2,1)} %bitcast.6, bf16[1,2048,768]{2,1,0:T(8,128)(2,1)} %param.15), kind=kOutput, calls=%fused_computation.27 | convolution fusion | flops 4831838208 | bytes 14155776 | tf_op jit(solution)/shard_map/dot_general | solution.py:8
  193.2 8.8 %fusion.7 = f32[1536,768]{1,0:T(8,128)S(1)} fusion(bf16[1536,2048]{1,0:T(8,128)(2,1)} %bitcast.6, bf16[1,2048,768]{2,1,0:T(8,128)(2,1)S(1)} %copy-done.5), kind=kOutput, calls=%fused_computation.23 | convolution fusion | flops 4831838208 | bytes 14155776 | tf_op jit(solution)/shard_map/dot_general | solution.py:9
  202.1 2.1 copy-done.9
  204.2 7.0 %convolution_convert_fusion = bf16[1536,2048]{1,0:T(8,128)(2,1)} fusion(bf16[1,768,2048]{2,1,0:T(8,128)(2,1)S(1)} %copy-done, f32[1536,768]{1,0:T(8,128)S(1)} %fusion.7, f32[1536,768]{1,0:T(8,128)S(1)} %fusion.11), kind=kOutput, calls=%fused_computation.13 | convolution fusion | flops 4842061824 | bytes 18874368 | tf_op jit(solution)/shard_map/dot_general | solution.py:16
  211.2 113.6 %all-to-all-done.2 = bf16[32,48,2048]{2,1,0:T(8,128)(2,1)} async-done(((bf16[32,48,2048]{2,1,0:T(8,128)(2,1)}), bf16[32,48,2048]{2,1,0:T(8,128)(2,1)}, u32[]{:S(2)}, u32[]{:S(2)}) %all-to-all-start.2) | async-done | bytes 6291488 | tf_op jit(solution)/shard_map/all_to_all | solution.py:84
  324.8 3.8 all-to-all-start.1
  328.7 8.7 %fusion.3 = f32[1536,768]{1,0:T(8,128)} fusion(bf16[1536,2048]{1,0:T(8,128)(2,1)} %bitcast.14, bf16[1,768,2048]{2,1,0:T(8,128)(2,1)S(1)} %copy-done), kind=kOutput, calls=%fused_computation.19 | convolution fusion | flops 4831838208 | bytes 14155776 | tf_op jit(solution)/shard_map/dot_general | solution.py:21
  337.5 13.1 %fusion.9 = f32[1536,2048]{1,0:T(8,128)} fusion(bf16[1,2048,768]{2,1,0:T(8,128)(2,1)S(1)} %copy-done.4, f32[1536,768]{1,0:T(8,128)S(1)} %copy-done.8, f32[1536,768]{1,0:T(8,128)} %fusion.3, f32[1536,768]{1,0:T(8,128)S(1)} %copy-done.10), kind=kOutput, calls=%fused_computation.25 | convolution fusion | flops 4843634688 | bytes 29884416 | tf_op jit(solution)/shard_map/dot_general | solution.py:26
  350.6 11.5 %add_convert_fusion = bf16[1536,2048]{1,0:T(8,128)(2,1)} fusion(f32[1536,2048]{1,0:T(8,128)} %fusion.9, bf16[1,2048,768]{2,1,0:T(8,128)(2,1)S(1)} %copy-done.6, f32[1536,768]{1,0:T(8,128)} %fusion.3, f32[1536,768]{1,0:T(8,128)S(1)} %copy-done.8), kind=kOutput, calls=%fused_computation.8 | convolution fusion | flops 4845207552 | bytes 31457280 | tf_op jit(solution)/shard_map/dot_general | solution.py:29
  362.1 106.4 %all-to-all-done.1 = bf16[32,48,2048]{2,1,0:T(8,128)(2,1)} async-done(((bf16[32,48,2048]{2,1,0:T(8,128)(2,1)}), bf16[32,48,2048]{2,1,0:T(8,128)(2,1)}, u32[]{:S(2)}, u32[]{:S(2)}) %all-to-all-start.1) | async-done | bytes 6291488 | tf_op jit(solution)/shard_map/all_to_all | solution.py:75
  468.5 4.0 all-to-all-start.3
  472.7 12.4 %gather_fusion.1 = bf16[1024,2048]{1,0:T(8,128)(2,1)} fusion(bf16[1536,2048]{1,0:T(8,128)(2,1)} %bitcast.11, s32[1024]{0:T(1024)S(1)} %broadcast_clamp_fusion), kind=kCustom, calls=%fused_computation.1 | custom fusion | bytes 8392704 | tf_op jit(solution)/shard_map/gather | solution.py:92
  485.1 5.7 fusion.2
  490.8 0.7 copy.29
  491.5 120.9 %all-to-all-done.3 = bf16[32,48,2048]{2,1,0:T(8,128)(2,1)} async-done(((bf16[32,48,2048]{2,1,0:T(8,128)(2,1)}), bf16[32,48,2048]{2,1,0:T(8,128)(2,1)}, u32[]{:S(2)}, u32[]{:S(2)}) %all-to-all-start.3) | async-done | bytes 6291488 | tf_op jit(solution)/shard_map/all_to_all | solution.py:88
  612.4 12.6 %gather_fusion.4 = bf16[1024,2048]{1,0:T(8,128)(2,1)} fusion(bf16[1536,2048]{1,0:T(8,128)(2,1)} %bitcast.16, s32[1024]{0:T(1024)S(1)} %broadcast_clamp_fusion), kind=kCustom, calls=%fused_computation.4 | custom fusion | bytes 8392704 | tf_op jit(solution)/shard_map/gather | solution.py:95
  625.0 5.9 bitcast_reduce_fusion
  (44 shorter events, 1.2 us)
Async XLA Ops:
  0.6 203.6 %copy-start = (bf16[1,768,2048]{2,1,0:T(8,128)(2,1)S(1)}, bf16[1,768,2048]{2,1,0:T(8,128)(2,1)}, u32[]{:S(2)}) copy-start(bf16[1,768,2048]{2,1,0:T(8,128)(2,1)} %param.17) | copy-start | bytes 9437188
  33.7 7.4 %copy-start.3 = (f32[128,8]{0,1:T(8,128)S(1)}, f32[128,8]{0,1:T(8,128)}, u32[]{:S(2)}) copy-start(f32[128,8]{0,1:T(8,128)} %param.11) | copy-start | bytes 12292
  33.7 147.4 %all-to-all-start = ((bf16[32,48,2048]{2,1,0:T(8,128)(2,1)}), bf16[32,48,2048]{2,1,0:T(8,128)(2,1)}, u32[]{:S(2)}, u32[]{:S(2)}) async-start(bf16[32,48,2048]{2,1,0:T(8,128)(2,1)} %bitcast.51), calls=%async_computation | async-start | bytes 12582912 | tf_op jit(solution)/shard_map/all_to_all | solution.py:71
  181.2 143.7 %all-to-all-start.2 = ((bf16[32,48,2048]{2,1,0:T(8,128)(2,1)}), bf16[32,48,2048]{2,1,0:T(8,128)(2,1)}, u32[]{:S(2)}, u32[]{:S(2)}) async-start(bf16[32,48,2048]{2,1,0:T(8,128)(2,1)} %fusion), calls=%async_computation.2 | async-start | bytes 12582912 | tf_op jit(solution)/shard_map/all_to_all | solution.py:84
  185.0 8.2 %copy-start.5 = (bf16[1,2048,768]{2,1,0:T(8,128)(2,1)S(1)}, bf16[1,2048,768]{2,1,0:T(8,128)(2,1)}, u32[]{:S(2)}) copy-start(bf16[1,2048,768]{2,1,0:T(8,128)(2,1)} %param.16) | copy-start | bytes 9437188
  193.2 8.9 %copy-start.7 = (f32[1536,768]{1,0:T(8,128)}, f32[1536,768]{1,0:T(8,128)S(1)}, u32[]{:S(2)}) copy-start(f32[1536,768]{1,0:T(8,128)S(1)} %fusion.11) | copy-start | bytes 14155780
  202.1 2.1 copy-start.9
  324.8 143.7 %all-to-all-start.1 = ((bf16[32,48,2048]{2,1,0:T(8,128)(2,1)}), bf16[32,48,2048]{2,1,0:T(8,128)(2,1)}, u32[]{:S(2)}, u32[]{:S(2)}) async-start(bf16[32,48,2048]{2,1,0:T(8,128)(2,1)} %bitcast.54), calls=%async_computation.1 | async-start | bytes 12582912 | tf_op jit(solution)/shard_map/all_to_all | solution.py:75
  328.7 8.7 %copy-start.4 = (bf16[1,2048,768]{2,1,0:T(8,128)(2,1)S(1)}, bf16[1,2048,768]{2,1,0:T(8,128)(2,1)}, u32[]{:S(2)}) copy-start(bf16[1,2048,768]{2,1,0:T(8,128)(2,1)} %param.15) | copy-start | bytes 9437188
  328.7 8.7 %copy-start.8 = (f32[1536,768]{1,0:T(8,128)S(1)}, f32[1536,768]{1,0:T(8,128)}, u32[]{:S(2)}) copy-start(f32[1536,768]{1,0:T(8,128)} %copy-done.7) | copy-start | bytes 14155780
  328.7 8.7 %copy-start.10 = (f32[1536,768]{1,0:T(8,128)S(1)}, f32[1536,768]{1,0:T(8,128)}, u32[]{:S(2)}) copy-start(f32[1536,768]{1,0:T(8,128)} %copy-done.9) | copy-start | bytes 14155780
  337.4 13.1 %copy-start.6 = (bf16[1,2048,768]{2,1,0:T(8,128)(2,1)S(1)}, bf16[1,2048,768]{2,1,0:T(8,128)(2,1)}, u32[]{:S(2)}) copy-start(bf16[1,2048,768]{2,1,0:T(8,128)(2,1)} %param.16) | copy-start | bytes 9437188
  468.5 4.0 copy-start.2
  468.5 143.8 %all-to-all-start.3 = ((bf16[32,48,2048]{2,1,0:T(8,128)(2,1)}), bf16[32,48,2048]{2,1,0:T(8,128)(2,1)}, u32[]{:S(2)}, u32[]{:S(2)}) async-start(bf16[32,48,2048]{2,1,0:T(8,128)(2,1)} %bitcast.53), calls=%async_computation.3 | async-start | bytes 12582912 | tf_op jit(solution)/shard_map/all_to_all | solution.py:88
  612.4 18.5 %copy-start.1 = (bf16[1,768,2048]{2,1,0:T(8,128)(2,1)S(1)}, bf16[1,768,2048]{2,1,0:T(8,128)(2,1)}, u32[]{:S(2)}) copy-start(bf16[1,768,2048]{2,1,0:T(8,128)(2,1)} %param.17) | copy-start | bytes 9437188
where the time goes:
time: 631 us
  waiting for transfers between devices  450 us (71%)
  local copies, waits for them, and re-layouts  74.4 us (12%)
  matrix products  57.4 us (9%)
  other arithmetic  29 us (5%)
  starting transfers between devices  19.1 us (3%)
    all_to_all x1, waiting for transfers between devices, body(): lax.all_to_all(pair_grad.reshape(cot_recv.shape), 'ep', split_axis=0, con...  121 us
    all_to_all x1, waiting for transfers between devices, body(): lax.all_to_all(send_c, 'ep', split_axis=0, concat_axis=0, tiled=True)  114 us
    all_to_all x1, waiting for transfers between devices, body(): lax.all_to_all(send_x, 'ep', split_axis=0, concat_axis=0, tiled=True)  109 us
    all_to_all x1, waiting for transfers between devices, body(): lax.all_to_all(out_rows.reshape(received.shape), 'ep', split_axis=0, conc...  106 us
    gather x1, local copies, waits for them, and re-layouts, body(): cot_pad[row_of].astype(jnp.float32) * gate_pad[source][:, None]  13.8 us
    gather x1, local copies, waits for them, and re-layouts, body(): send_x = tok_pad[row_of].reshape(count, slots, width)  13.8 us
    dot_general x1, matrix products, project_back(): lax.dot_general(grad_a, wg, (((1,), (1,)), ((), ())), preferred_element_t...  13.1 us
  transfers between devices with their start and end apart: 4, of which 4 were waited for; matrix products, arithmetic and copies ran while one was open for 17% of the time, Pallas kernels for 0%

commit v1 on v0

v1 whole, which is shorter than its diff:
```python
import jax
import jax.numpy as jnp
from jax import lax
from jax.sharding import PartitionSpec as P


def body(tokens, cotangent, gates, experts, owner, swapped, w_gate, w_up, w_down):
    tok_rows, width = tokens.shape
    top_count = experts.shape[1]
    expert_total = owner.shape[0]
    count = lax.axis_size("ep")
    slots = tok_rows * top_count * 3 // (2 * expert_total)
    f32, bf16 = jnp.float32, jnp.bfloat16
    devices = jnp.arange(count, dtype=jnp.int32)
    dev_flag = jnp.repeat(swapped, 2)
    step_dev = dev_flag * (1 - 2 * (devices % 2))
    holder = owner + jnp.sum(
        jnp.where(owner[:, None] == devices[None, :], step_dev[None, :], 0), axis=1
    )
    wg, wu, wd = w_gate[0], w_up[0], w_down[0]
    tok_all = lax.all_gather(tokens, "ep", axis=0, tiled=False)
    cot_all = lax.all_gather(cotangent, "ep", axis=0, tiled=False)
    held = jnp.sum(
        jnp.where(holder[None, :] == devices[:, None], jnp.arange(expert_total, dtype=jnp.int32)[None, :], 0),
        axis=1,
    )
    hit = experts[None, :, :] == held[:, None, None]
    weight = jnp.sum(jnp.where(hit, gates[None, :, :], 0.0), axis=2)
    weight = lax.all_to_all(weight, "ep", split_axis=0, concat_axis=0, tiled=True)
    mask = weight > 0.0
    at = jnp.arange(tok_rows, dtype=jnp.int32)
    before = (at[:, None] < at[None, :]).astype(bf16)
    rank = jnp.dot(mask.astype(bf16), before, preferred_element_type=f32).astype(jnp.int32)
    rank = jnp.where(mask, rank, -1)
    pick = rank[:, None, :] == jnp.arange(slots, dtype=jnp.int32)[None, :, None]
    w_rows = jnp.sum(jnp.where(pick, weight[:, None, :], 0.0), axis=2).reshape(-1, 1)
    pick = pick.astype(bf16)

    def gather(x):
        return lax.dot_general(
            pick, x, (((2,), (1,)), ((0,), (0,))), preferred_element_type=f32
        ).astype(bf16).reshape(-1, width)

    def spread(rows):
        return lax.dot_general(
            pick, rows.reshape(count, slots, width), (((1,), (1,)), ((0,), (0,))), preferred_element_type=f32
        ).astype(bf16)

    x = gather(tok_all)
    c = gather(cot_all)
    a = jnp.dot(x, wg, preferred_element_type=f32)
    b = jnp.dot(x, wu, preferred_element_type=f32)
    sig = jax.nn.sigmoid(a)
    hidden = (a * sig * b).astype(bf16)
    out = jnp.dot(hidden, wd, preferred_element_type=f32).astype(bf16).astype(f32)
    mixed = spread((w_rows * out).astype(bf16))
    mixed = lax.psum_scatter(mixed, "ep", scatter_dimension=0, tiled=False)
    cf = c.astype(f32)
    gg = jnp.sum(cf * out, axis=1).reshape(count, slots)
    gg = jnp.sum(jnp.where(pick > 0, gg[:, :, None], 0.0), axis=1)
    gg = lax.all_to_all(gg, "ep", split_axis=0, concat_axis=0, tiled=True)
    gate_grad = jnp.sum(jnp.where(hit, gg[:, :, None], 0.0), axis=0)
    cs = (cf * w_rows).astype(bf16)
    bh = lax.dot_general(cs, wd, (((1,), (1,)), ((), ())), preferred_element_type=f32)
    ga = (bh * b * sig * (1.0 + a * (1.0 - sig))).astype(bf16)
    gb = (bh * a * sig).astype(bf16)
    pg = lax.dot_general(ga, wg, (((1,), (1,)), ((), ())), preferred_element_type=f32)
    pg = pg + lax.dot_general(gb, wu, (((1,), (1,)), ((), ())), preferred_element_type=f32)
    in_grad = lax.psum_scatter(spread(pg.astype(bf16)), "ep", scatter_dimension=0, tiled=False)
    return (mixed, in_grad, gate_grad)


def solution(mesh):
    return jax.shard_map(
        body,
        mesh=mesh,
        in_specs=(
            P("ep", None),
            P("ep", None),
            P("ep", None),
            P("ep", None),
            P(),
            P(),
            P("ep", None, None),
            P("ep", None, None),
            P("ep", None, None),
        ),
        out_specs=(P("ep", None), P("ep", None), P("ep", None)),
        check_vma=False,
    )
```

time: 631 us -> 700 us (1.11)
  waiting for transfers between devices: 450 us -> 537 us
  local copies, waits for them, and re-layouts: 74.4 us -> 3.13 us
  matrix products: 57.4 us -> 103 us
  blocking collectives: 0 us -> 24.1 us
  starting transfers between devices: 19.1 us -> 0.38 us
  between operations: 0.92 us -> 13.9 us
  other arithmetic: 29 us -> 18.2 us
    all_to_all x4 -> x0, waiting for transfers between devices: 450 us -> none  [the longest x1 121 us: body(): lax.all_to_all(pair_grad.reshape(cot_recv.shape), 'ep', split_axis=0, con...]
    reduce_scatter x0 -> x2, waiting for transfers between devices: none -> 339 us  [the longest x1 188 us: body(): mixed = lax.psum_scatter(mixed, 'ep', scatter_dimension=0, tiled=False)]
    all_gather x0 -> x2, waiting for transfers between devices: none -> 196 us  [the longest x1 102 us: body(): tok_all = lax.all_gather(tokens, 'ep', axis=0, tiled=False)]
    gather x5 -> x0, local copies, waits for them, and re-layouts: 61 us -> none  [the longest x1 13.8 us: body(): cot_pad[row_of].astype(jnp.float32) * gate_pad[source][:, None]]
    dot_general x6 -> x11, matrix products: 57.4 us -> 103 us  [the longest x2 26.1 us: spread(): lax.dot_general(pick, rows.reshape(count, slots, width), (((1,), (1,)), (...]
    all_to_all x0 -> x2, blocking collectives: none -> 24.1 us  [the longest x1 14.3 us: body(): lax.all_to_all(weight, 'ep', split_axis=0, concat_axis=0, tiled=True)]
    all_to_all x4 -> x0, starting transfers between devices: 19.1 us -> none  [the longest x1 7.41 us: body(): lax.all_to_all(send_x, 'ep', split_axis=0, concat_axis=0, tiled=True)]
    reduce_sum x4, other arithmetic: 11.7 us -> 2.2 us  [the longest x1 0.82 us: body(): weight = jnp.sum(jnp.where(hit, gates[None, :, :], 0.0), axis=2)]
  transfers between devices with their start and end apart: 4 -> 4, of which waited for: 4 -> 4; matrix products, arithmetic and copies ran while one was open for 17% -> 6% of each run, Pallas kernels for 0% -> 0%
where the time goes in v1:
time: 700 us; the launch traced here: 699 us
  waiting for transfers between devices  537 us (77%)
  matrix products  103 us (15%)
  blocking collectives  24.1 us (3%)
  other arithmetic  18.2 us (3%)
  between operations  13.9 us (2%)
    reduce_scatter x1, waiting for transfers between devices, body(): mixed = lax.psum_scatter(mixed, 'ep', scatter_dimension=0, tiled=False)  188 us
    reduce_scatter x1, waiting for transfers between devices, body(): lax.psum_scatter(spread(pg.astype(bf16)), 'ep', scatter_dimension=0, tile...  151 us
    all_gather x1, waiting for transfers between devices, body(): tok_all = lax.all_gather(tokens, 'ep', axis=0, tiled=False)  102 us
    all_gather x1, waiting for transfers between devices, body(): cot_all = lax.all_gather(cotangent, 'ep', axis=0, tiled=False)  94.4 us
    dot_general x2, matrix products, spread(): lax.dot_general(pick, rows.reshape(count, slots, width), (((1,), (1,)), (...  26.1 us
    dot_general x1, matrix products, body(): jnp.dot(hidden, wd, preferred_element_type=f32).astype(bf16).astype(f32)  15.9 us
    dot_general x2, matrix products, gather(): lax.dot_general(pick, x, (((2,), (1,)), ((0,), (0,))), preferred_element_...  15.2 us
    all_to_all x1, blocking collectives, body(): lax.all_to_all(weight, 'ep', split_axis=0, concat_axis=0, tiled=True)  14.3 us
  transfers between devices with their start and end apart: 4, of which 4 were waited for; matrix products, arithmetic and copies ran while one was open for 6% of the time, Pallas kernels for 0%

profile of v1, /device:TPU:0, one launch (start us, length us, event | category | flops | bytes accessed | tf_op | source)
XLA Modules:
  0.0 699.4 jit_solution(6147909657517877664)
XLA Ops:
  7.2 0.7 all-gather.5.cloned.1.call-update
  8.0 0.7 all-gather.7.cloned.1.call-update
  8.7 0.7 broadcast_in_dim.86
  9.4 0.1 reshape.60
  9.5 0.8 select_reduce_fusion.3
  10.4 0.7 add.27
  11.0 0.1 select_reduce_fusion.2
  11.2 0.8 fusion.21
  12.0 14.3 %all_to_all.21 = f32[32,1,128]{2,1,0:T(1,128)S(1)} all-to-all(f32[32,1,128]{2,1,0:T(1,128)S(1)} %bitcast.51), channel_id=1, replica_groups=mesh['ep'=32] {'ep'}, dimensions={0} | all-to-all | bytes 32768 | tf_op jit(solution)/shard_map/all_to_all | solution.py:29
  26.2 0.1 fusion.15
  26.4 102.1 %all-gather.5.cloned.1.call-done = bf16[4096,2048]{1,0:T(8,128)(2,1)} async-done(((bf16[128,2048]{1,0:T(8,128)(2,1)}), bf16[4096,2048]{1,0:T(8,128)(2,1)}) %all-gather.5.cloned.1.call-update) | async-done | bytes 16777232 | tf_op jit(solution)/shard_map/all_gather | solution.py:21
  128.5 8.2 %convolution_convert_fusion.3 = bf16[32,48,2048]{2,1,0:T(8,128)(2,1)S(1)} fusion(bf16[32,128,2048]{2,1,0:T(8,128)(2,1)} %bitcast.40, s32[32,128]{1,0:T(8,128)S(1)} %fusion.15), kind=kOutput, calls=%fused_computation.14 | convolution fusion | flops 808648704 | bytes 23085056 | tf_op jit(solution)/shard_map/dot_general | solution.py:40
  136.7 6.7 fusion.10
  143.4 6.6 fusion.6
  150.0 94.4 %all-gather.7.cloned.1.call-done = bf16[4096,2048]{1,0:T(8,128)(2,1)} async-done(((bf16[128,2048]{1,0:T(8,128)(2,1)}), bf16[4096,2048]{1,0:T(8,128)(2,1)}) %all-gather.7.cloned.1.call-update) | async-done | bytes 16777232 | tf_op jit(solution)/shard_map/all_gather | solution.py:22
  244.4 7.0 %convert_convert_fusion = f32[32,48,2048]{2,1,0:T(8,128)S(1)} fusion(bf16[32,128,2048]{2,1,0:T(8,128)(2,1)} %bitcast.41, s32[32,128]{1,0:T(8,128)S(1)} %fusion.15), kind=kOutput, calls=%fused_computation.9 | convolution fusion | flops 811794432 | bytes 29376512 | tf_op jit(solution)/shard_map/dot_general | solution.py:40
  251.4 15.9 %fusion.1 = (f32[1536]{0:T(1024)S(1)}, bf16[1536,2048]{1,0:T(8,128)(2,1)}) fusion(f32[32,48,2048]{2,1,0:T(8,128)S(1)} %convert_convert_fusion, bf16[1,768,2048]{2,1,0:T(8,128)(2,1)S(1)} %copy-done, f32[1536,768]{1,0:T(8,128)} %fusion.6, f32[1536,768]{1,0:T(8,128)} %fusion.10), kind=kOutput, calls=%fused_computation.5 | convolution fusion | flops 4851497472 | bytes 31463424 | tf_op jit(solution)/shard_map/dot_general | solution.py:55
  267.4 0.6 select_reduce_fusion
  268.0 8.0 %multiply_convert_fusion = bf16[32,48,2048]{2,1,0:T(8,128)(2,1)} fusion(f32[32,48,2048]{2,1,0:T(8,128)} %copy-done.2, f32[32,48]{1,0:T(8,128)S(1)} %get-tuple-element.4), kind=kLoop, calls=%fused_computation.7 | loop fusion | flops 6291456 | bytes 18880512 | tf_op jit(solution)/shard_map/convert_element_type | solution.py:63
  276.0 7.3 %fusion.2 = f32[1536,768]{1,0:T(8,128)S(1)} fusion(bf16[1536,2048]{1,0:T(8,128)(2,1)} %bitcast.46, bf16[1,768,2048]{2,1,0:T(8,128)(2,1)S(1)} %copy-done), kind=kOutput, calls=%fused_computation.15 | convolution fusion | flops 4831838208 | bytes 14155776 | tf_op jit(solution)/shard_map/dot_general | solution.py:64
  283.4 2.1 copy-done.8
  285.5 13.4 %fusion.8 = f32[1536,2048]{1,0:T(8,128)} fusion(bf16[1,2048,768]{2,1,0:T(8,128)(2,1)S(1)} %copy-done.5, f32[1536,768]{1,0:T(8,128)S(1)} %bitcast.55, f32[1536,768]{1,0:T(8,128)S(1)} %fusion.2, f32[1536,768]{1,0:T(8,128)} %fusion.6), kind=kOutput, calls=%fused_computation.21 | convolution fusion | flops 4843634688 | bytes 29884416 | tf_op jit(solution)/shard_map/dot_general | solution.py:67
  298.9 11.7 %add_convert_fusion = bf16[1536,2048]{1,0:T(8,128)(2,1)} fusion(f32[1536,2048]{1,0:T(8,128)} %fusion.8, bf16[1,2048,768]{2,1,0:T(8,128)(2,1)S(1)} %copy-done.7, f32[1536,768]{1,0:T(8,128)} %copy-done.8, f32[1536,768]{1,0:T(8,128)S(1)} %bitcast.55), kind=kOutput, calls=%fused_computation.6 | convolution fusion | flops 4845207552 | bytes 31457280 | tf_op jit(solution)/shard_map/dot_general | solution.py:68
  310.6 13.0 %convolution_convert_fusion = bf16[32,128,2048]{2,1,0:T(8,128)(2,1)} fusion(bf16[32,48,2048]{2,1,0:T(8,128)(2,1)} %bitcast.45, s32[32,128]{1,0:T(8,128)S(1)} %fusion.15), kind=kOutput, calls=%fused_computation.2 | convolution fusion | flops 813891584 | bytes 23085056 | tf_op jit(solution)/shard_map/dot_general | solution.py:45
  323.6 0.3 reduce-scatter.3.cloned.1.call-start
  323.9 0.1 mul.63
  324.0 6.5 fusion
  330.4 13.1 %convolution_convert_fusion.1 = bf16[32,128,2048]{2,1,0:T(8,128)(2,1)} fusion(bf16[32,48,2048]{2,1,0:T(8,128)(2,1)} %bitcast.42, s32[32,128]{1,0:T(8,128)S(1)} %fusion.15), kind=kOutput, calls=%fused_computation.3 | convolution fusion | flops 813891584 | bytes 23085056 | tf_op jit(solution)/shard_map/dot_general | solution.py:45
  343.5 9.8 %all_to_all.22 = f32[32,1,128]{2,1,0:T(1,128)S(1)} all-to-all(f32[32,1,128]{2,1,0:T(1,128)S(1)} %bitcast.49), channel_id=1, replica_groups=mesh['ep'=32] {'ep'}, dimensions={0} | all-to-all | bytes 32768 | tf_op jit(solution)/shard_map/all_to_all | solution.py:61
  353.4 0.7 fusion.22
  354.1 151.0 %reduce-scatter.5.cloned.1.call-done = bf16[1,128,2048]{2,1,0:T(8,128)(2,1)} async-done(((bf16[32,128,2048]{2,1,0:T(8,128)(2,1)}), bf16[1,128,2048]{2,1,0:T(8,128)(2,1)}) %reduce-scatter.5.cloned.1.call-update) | async-done | bytes 524304 | tf_op jit(solution)/shard_map/reduce_scatter | solution.py:69
  505.0 187.9 %reduce-scatter.3.cloned.1.call-done = bf16[1,128,2048]{2,1,0:T(8,128)(2,1)} async-done(((bf16[32,128,2048]{2,1,0:T(8,128)(2,1)}), bf16[1,128,2048]{2,1,0:T(8,128)(2,1)}) %reduce-scatter.3.cloned.1.call-update) | async-done | bytes 524304 | tf_op jit(solution)/shard_map/reduce_scatter | solution.py:57
  (29 shorter events, 0.3 us)
Async XLA Ops:
  7.2 244.2 %copy-start = (bf16[1,768,2048]{2,1,0:T(8,128)(2,1)S(1)}, bf16[1,768,2048]{2,1,0:T(8,128)(2,1)}, u32[]{:S(2)}) copy-start(bf16[1,768,2048]{2,1,0:T(8,128)(2,1)} %param.17) | copy-start | bytes 9437188
  7.2 121.3 %all-gather.5.cloned.1.call-start = ((), (), s32[]{:S(2)}) async-start(), calls=%async_computation.6 | async-start | bytes 17301504 | tf_op jit(solution)/shard_map/all_gather | solution.py:21
  7.9 236.5 %all-gather.7.cloned.1.call-start = ((), (), s32[]{:S(2)}) async-start(), calls=%async_computation.7 | async-start | bytes 17301504 | tf_op jit(solution)/shard_map/all_gather | solution.py:22
  8.7 496.3 %reduce-scatter.5.cloned.1.call-start = ((), (), s32[]{:S(2)}) async-start(), calls=%async_computation.5 | async-start | bytes 17301504 | tf_op jit(solution)/shard_map/reduce_scatter | solution.py:69
  128.5 8.2 %copy-start.4 = (bf16[1,2048,768]{2,1,0:T(8,128)(2,1)S(1)}, bf16[1,2048,768]{2,1,0:T(8,128)(2,1)}, u32[]{:S(2)}) copy-start(bf16[1,2048,768]{2,1,0:T(8,128)(2,1)} %param.15) | copy-start | bytes 9437188
  136.7 6.7 copy-start.6
  251.4 15.9 %copy-start.2 = (f32[32,48,2048]{2,1,0:T(8,128)}, f32[32,48,2048]{2,1,0:T(8,128)S(1)}, u32[]{:S(2)}) copy-start(f32[32,48,2048]{2,1,0:T(8,128)S(1)} %convert_convert_fusion) | copy-start | bytes 37748740
  268.0 17.5 %slice-start = ((s8[4718592]{0:T(1024)(128)(4,1)}), s8[524288]{0:T(1024)(128)(4,1)S(1)}, s32[]{:S(2)}) async-start(s8[4718592]{0:T(1024)(128)(4,1)} %bitcast.54), calls=%async_computation.8 | async-start | bytes 1048576
  276.0 9.5 %copy-start.5 = (bf16[1,2048,768]{2,1,0:T(8,128)(2,1)S(1)}, bf16[1,2048,768]{2,1,0:T(8,128)(2,1)}, u32[]{:S(2)}) copy-start(bf16[1,2048,768]{2,1,0:T(8,128)(2,1)} %param.15) | copy-start | bytes 9437188
  276.0 9.5 %slice-start.1 = ((s8[4718592]{0:T(1024)(128)(4,1)}), s8[4194304]{0:T(1024)(128)(4,1)S(1)}, s32[]{:S(2)}) async-start(s8[4718592]{0:T(1024)(128)(4,1)} %bitcast.54), calls=%async_computation.9 | async-start | bytes 8388608
  283.4 2.1 copy-start.8
  285.5 13.4 %copy-start.7 = (bf16[1,2048,768]{2,1,0:T(8,128)(2,1)S(1)}, bf16[1,2048,768]{2,1,0:T(8,128)(2,1)}, u32[]{:S(2)}) copy-start(bf16[1,2048,768]{2,1,0:T(8,128)(2,1)} %param.16) | copy-start | bytes 9437188
  323.6 369.2 %reduce-scatter.3.cloned.1.call-start = ((), (), s32[]{:S(2)}) async-start(), calls=%async_computation.4 | async-start | bytes 17301504 | tf_op jit(solution)/shard_map/reduce_scatter | solution.py:57
  343.5 349.4 %copy-start.1 = (bf16[1,768,2048]{2,1,0:T(8,128)(2,1)S(1)}, bf16[1,768,2048]{2,1,0:T(8,128)(2,1)}, u32[]{:S(2)}) copy-start(bf16[1,768,2048]{2,1,0:T(8,128)(2,1)} %param.17) | copy-start | bytes 9437188
  343.5 9.8 %copy-start.3 = (s32[128,8]{0,1:T(8,128)S(1)}, s32[128,8]{0,1:T(8,128)}, u32[]{:S(2)}) copy-start(s32[128,8]{0,1:T(8,128)} %param.12) | copy-start | bytes 12292
Sparse Core Ops, SparseCore 0:
  10.9 117.5 all-gather.4
  131.3 113.0 all-gather.6
  323.8 181.1 reduce-scatter.4
  507.7 185.0 reduce-scatter.2

commit v2 on v1

--- a/solution.py
+++ b/solution.py
@@ -1,7 +1,273 @@
+import functools
+
 import jax
 import jax.numpy as jnp
 from jax import lax
+from jax.experimental import pallas as pl
+from jax.experimental.pallas import tpu as pltpu
 from jax.sharding import PartitionSpec as P
+
+NZ = 4
+MESH = pl.DeviceIdType.MESH
+
+
+def places():
+    me = lax.axis_index("ep")
+    return me // 8, lax.rem(me // 4, 2), lax.rem(me // 2, 2), lax.rem(me, 2)
+
+
+def at_place(z, y, x, c):
+    return ((z * 2 + y) * 2 + x) * 2 + c
+
+
+def greet(peers):
+    barrier = pltpu.get_barrier_semaphore()
+    for peer in peers:
+        pl.semaphore_signal(barrier, inc=1, device_id=(peer,), device_id_type=MESH)
+    pl.semaphore_wait(barrier, len(peers))
+
+
+def gather_kernel(n, *refs):
+    ins, outs = refs[:n], refs[n : 2 * n]
+    send, recv, local = refs[2 * n :]
+    z, y, x, c = places()
+    rows = ins[0].shape[0]
+    half = rows // 2
+    me = at_place(z, y, x, c)
+    xp, yp = at_place(z, y, 1 - x, c), at_place(z, 1 - y, x, c)
+    sib = at_place(z, y, x, 1 - c)
+
+    def zi(d):
+        return lax.rem(z + NZ + d, NZ)
+
+    zp = {d: at_place(zi(d), y, x, c) for d in (1, 2, 3)}
+    greet([zp[1], zp[2], zp[3], xp, yp, sib])
+
+    def origin(q, d, core):
+        return at_place(zi(-d), 1 - y if "y" in q else y, 1 - x if "x" in q else x, core)
+
+    def copy(t, role, where, cut, dev, own=False):
+        src = ins[t] if own else outs[t].at[where]
+        dst = outs[t].at[where]
+        if cut is not None:
+            src, dst = src.at[pl.ds(cut * half, half)], dst.at[pl.ds(cut * half, half)]
+        return pltpu.make_async_remote_copy(
+            src_ref=src,
+            dst_ref=dst,
+            send_sem=send.at[t, role],
+            recv_sem=recv.at[t, role],
+            device_id=(dev,),
+            device_id_type=MESH,
+        )
+
+    Z, Y, X, XY, YX, S = 0, 4, 8, 12, 16, 20
+    Q = {"o": 0, "y": 4, "x": 8, "xy": 12}
+    sent = []
+
+    def go(*args, **kw):
+        cp = copy(*args, **kw)
+        cp.start()
+        sent.append(cp)
+
+    def to_sib(t, q, d):
+        go(t, S + Q[q] + d, origin(q, d, c), None, sib, own=(q == "o" and d == 0))
+
+    def arrived(t, role, where, cut=None):
+        copy(t, role, where, cut, sib).wait_recv()
+
+    locals_ = []
+    for t in range(n):
+        for d in (2, 1, 3):
+            go(t, Z + d, me, None, zp[d], own=True)
+        go(t, Y, me, None, yp, own=True)
+        go(t, X, me, None, xp, own=True)
+        to_sib(t, "o", 0)
+        cp = pltpu.make_async_copy(ins[t], outs[t].at[me], local.at[t])
+        cp.start()
+        locals_.append(cp)
+    for t in range(n):
+        for d in (0, 1, 3, 2):
+            if d:
+                arrived(t, Z + d, origin("o", d, c))
+                go(t, Y + d, origin("o", d, c), None, yp)
+                go(t, X + d, origin("o", d, c), None, xp)
+                to_sib(t, "o", d)
+        for d in (0, 1, 3, 2):
+            arrived(t, Y + d, origin("y", d, c))
+            go(t, XY + d, origin("y", d, c), 0, xp)
+            to_sib(t, "y", d)
+            arrived(t, X + d, origin("x", d, c))
+            go(t, YX + d, origin("x", d, c), 1, yp)
+            to_sib(t, "x", d)
+    for t in range(n):
+        for d in (0, 1, 3, 2):
+            arrived(t, XY + d, origin("xy", d, c), 0)
+            arrived(t, YX + d, origin("xy", d, c), 1)
+            to_sib(t, "xy", d)
+    for t in range(n):
+        for q in Q:
+            for d in range(NZ):
+                arrived(t, S + Q[q] + d, origin(q, d, 1 - c))
+    for cp in locals_:
+        cp.wait()
+    for cp in sent:
+        cp.wait_send()
+
+
+def gather_blocks(*xs):
+    n = len(xs)
+    count = lax.axis_size("ep")
+    if count != 32:
+        return [lax.all_gather(v, "ep", axis=0, tiled=False) for v in xs]
+    return pl.pallas_call(
+        functools.partial(gather_kernel, n),
+        out_shape=[jax.ShapeDtypeStruct((count,) + v.shape, v.dtype) for v in xs],
+        in_specs=[pl.BlockSpec(memory_space=pl.ANY)] * n,
+        out_specs=[pl.BlockSpec(memory_space=pl.ANY)] * n,
+        scratch_shapes=[
+            pltpu.SemaphoreType.DMA((n, 36)),
+            pltpu.SemaphoreType.DMA((n, 36)),
+            pltpu.SemaphoreType.DMA((n,)),
+        ],
+        compiler_params=pltpu.CompilerParams(collective_id=0, has_side_effects=True),
+        cost_estimate=pl.CostEstimate(flops=0, bytes_accessed=n * 32 * xs[0].size * 2, transcendentals=0),
+    )(*xs)
+
+
+def scatter_kernel(n, *refs):
+    ins, outs = refs[:n], refs[n : 2 * n]
+    acc, r0, r1, r2, r3, send, recv, local = refs[2 * n :]
+    z, y, x, c = places()
+    rows, width = outs[0].shape
+    half = rows // 2
+    step = 16
+    f32 = jnp.float32
+    xp, yp = at_place(z, y, 1 - x, c), at_place(z, 1 - y, x, c)
+    sib = at_place(z, y, x, 1 - c)
+
+    def zi(d):
+        return lax.rem(z + d, NZ)
+
+    zp = {d: at_place(zi(d), y, x, c) for d in (1, 2, 3)}
+    greet([zp[1], zp[2], zp[3], xp, yp, sib])
+    Q = {"o": 0, "y": 4, "x": 8, "xy": 12}
+    A1, A2, Z = 16, 32, 40
+
+    def block(q, d, core):
+        return at_place(zi(d), 1 - y if "y" in q else y, 1 - x if "x" in q else x, core)
+
+    def copy(t, role, src, dst, dev):
+        return pltpu.make_async_remote_copy(
+            src_ref=src,
+            dst_ref=dst,
+            send_sem=send.at[t, role],
+            recv_sem=recv.at[t, role],
+            device_id=(dev,),
+            device_id_type=MESH,
+        )
+
+    sent = []
+
+    def go(*args):
+        cp = copy(*args)
+        cp.start()
+        sent.append(cp)
+
+    def arrived(t, role, dst, dev):
+        copy(t, role, dst, dst, dev).wait_recv()
+
+    def add(dst, terms, lo, size):
+        @pl.loop(0, size // step)
+        def _(i):
+            at = pl.ds(pl.multiple_of(lo + i * step, step), step)
+            there = pl.ds(pl.multiple_of(i * step, step), step)
+            total = None
+            for term, whole in terms:
+                v = term[at if whole else there, :].astype(f32)
+                total = v if total is None else total + v
+            dst[at, :] = total.astype(dst.dtype)
+
+    order = [(t, d) for t in range(n) for d in (2, 1, 3, 0)]
+    for t, d in order:
+        for q in ("xy", "x", "y", "o"):
+            go(t, Q[q] + d, ins[t].at[block(q, d, 1 - c)], r0.at[t, Q[q] + d], sib)
+            pltpu.make_async_copy(ins[t].at[block(q, d, c)], acc.at[t, Q[q] + d], local.at[t, Q[q] + d]).start()
+
+    def stage0(t, d):
+        for q in ("xy", "x", "y", "o"):
+            s = Q[q] + d
+            pltpu.make_async_copy(ins[t].at[block(q, d, c)], acc.at[t, s], local.at[t, s]).wait()
+            arrived(t, s, r0.at[t, s], sib)
+            add(acc.at[t, s], [(acc.at[t, s], True), (r0.at[t, s], True)], 0, rows)
+            first, second = acc.at[t, s, pl.ds(0, half)], acc.at[t, s, pl.ds(half, half)]
+            if q == "xy":
+                go(t, A1 + 4 + d, first, r1.at[t, 4 + d], xp)
+                go(t, A1 + 12 + d, second, r1.at[t, 12 + d], yp)
+            elif q == "x":
+                go(t, A1 + d, first, r1.at[t, d], xp)
+            elif q == "y":
+                go(t, A1 + 8 + d, second, r1.at[t, 8 + d], yp)
+
+    def stage1(t, d):
+        sy, sx = Q["y"] + d, Q["x"] + d
+        arrived(t, A1 + 4 + d, r1.at[t, 4 + d], xp)
+        add(acc.at[t, sy], [(acc.at[t, sy], True), (r1.at[t, 4 + d], False)], 0, half)
+        go(t, A2 + d, acc.at[t, sy, pl.ds(0, half)], r2.at[t, d], yp)
+        arrived(t, A1 + 12 + d, r1.at[t, 12 + d], yp)
+        add(acc.at[t, sx], [(acc.at[t, sx], True), (r1.at[t, 12 + d], False)], half, half)
+        go(t, A2 + 4 + d, acc.at[t, sx, pl.ds(half, half)], r2.at[t, 4 + d], xp)
+
+    def stage2(t, d):
+        arrived(t, A1 + d, r1.at[t, d], xp)
+        arrived(t, A2 + d, r2.at[t, d], yp)
+        add(acc.at[t, d], [(acc.at[t, d], True), (r1.at[t, d], False), (r2.at[t, d], False)], 0, half)
+        arrived(t, A1 + 8 + d, r1.at[t, 8 + d], yp)
+        arrived(t, A2 + 4 + d, r2.at[t, 4 + d], xp)
+        add(acc.at[t, d], [(acc.at[t, d], True), (r1.at[t, 8 + d], False), (r2.at[t, 4 + d], False)], half, half)
+        if d:
+            go(t, Z + d, acc.at[t, d], r3.at[t, d - 1], zp[d])
+
+    for k in range(len(order) + 2):
+        if k < len(order):
+            stage0(*order[k])
+        if 1 <= k < len(order) + 1:
+            stage1(*order[k - 1])
+        if k >= 2:
+            stage2(*order[k - 2])
+    for t in range(n):
+        for d in (1, 2, 3):
+            arrived(t, Z + d, r3.at[t, d - 1], zp[d])
+        add(outs[t], [(acc.at[t, 0], True)] + [(r3.at[t, d], True) for d in range(3)], 0, rows)
+    for cp in sent:
+        cp.wait_send()
+
+
+def scatter_sums(*xs):
+    n = len(xs)
+    count, rows, width = xs[0].shape
+    if count != 32:
+        return [lax.psum_scatter(v, "ep", scatter_dimension=0, tiled=False) for v in xs]
+    bf16 = jnp.bfloat16
+    return pl.pallas_call(
+        functools.partial(scatter_kernel, n),
+        out_shape=[jax.ShapeDtypeStruct((rows, width), bf16) for v in xs],
+        in_specs=[pl.BlockSpec(memory_space=pl.ANY)] * n,
+        out_specs=[pl.BlockSpec(memory_space=pltpu.VMEM)] * n,
+        scratch_shapes=[
+            pltpu.VMEM((n, 16, rows, width), bf16),
+            pltpu.VMEM((n, 16, rows, width), bf16),
+            pltpu.VMEM((n, 16, rows // 2, width), bf16),
+            pltpu.VMEM((n, 8, rows // 2, width), bf16),
+            pltpu.VMEM((n, 3, rows, width), bf16),
+            pltpu.SemaphoreType.DMA((n, 44)),
+            pltpu.SemaphoreType.DMA((n, 44)),
+            pltpu.SemaphoreType.DMA((n, 16)),
+        ],
+        compiler_params=pltpu.CompilerParams(
+            collective_id=1, has_side_effects=True, vmem_limit_bytes=58 << 20
+        ),
+        cost_estimate=pl.CostEstimate(flops=0, bytes_accessed=n * 32 * rows * width * 2, transcendentals=0),
+    )(*xs)
 
 
 def body(tokens, cotangent, gates, experts, owner, swapped, w_gate, w_up, w_down):
@@ -18,8 +284,7 @@
         jnp.where(owner[:, None] == devices[None, :], step_dev[None, :], 0), axis=1
     )
     wg, wu, wd = w_gate[0], w_up[0], w_down[0]
-    tok_all = lax.all_gather(tokens, "ep", axis=0, tiled=False)
-    cot_all = lax.all_gather(cotangent, "ep", axis=0, tiled=False)
+    tok_all, cot_all = gather_blocks(tokens, cotangent)
     held = jnp.sum(
         jnp.where(holder[None, :] == devices[:, None], jnp.arange(expert_total, dtype=jnp.int32)[None, :], 0),
         axis=1,
@@ -54,7 +319,6 @@
     hidden = (a * sig * b).astype(bf16)
     out = jnp.dot(hidden, wd, preferred_element_type=f32).astype(bf16).astype(f32)
     mixed = spread((w_rows * out).astype(bf16))
-    mixed = lax.psum_scatter(mixed, "ep", scatter_dimension=0, tiled=False)
     cf = c.astype(f32)
     gg = jnp.sum(cf * out, axis=1).reshape(count, slots)
     gg = jnp.sum(jnp.where(pick > 0, gg[:, :, None], 0.0), axis=1)
@@ -66,7 +330,7 @@
     gb = (bh * a * sig).astype(bf16)
     pg = lax.dot_general(ga, wg, (((1,), (1,)), ((), ())), preferred_element_type=f32)
     pg = pg + lax.dot_general(gb, wu, (((1,), (1,)), ((), ())), preferred_element_type=f32)
-    in_grad = lax.psum_scatter(spread(pg.astype(bf16)), "ep", scatter_dimension=0, tiled=False)
+    mixed, in_grad = scatter_sums(mixed, spread(pg.astype(bf16)))
     return (mixed, in_grad, gate_grad)
 
 

time: 700 us -> 474 us (0.68)
  waiting for transfers between devices: 537 us -> 0.01 us
  Pallas kernels: 0 us -> 300 us
  starting transfers between devices: 0.38 us -> 42.9 us
  blocking collectives: 24.1 us -> 0 us
  between operations: 13.9 us -> 0.78 us
    reduce_scatter x2 -> x0, waiting for transfers between devices: 339 us -> none  [the longest x1 188 us: body(): mixed = lax.psum_scatter(mixed, 'ep', scatter_dimension=0, tiled=False)]
    pallas_call x0 -> x2, Pallas kernels: none -> 300 us  [the longest x1 154 us: scatter_sums(): pl.pallas_call(functools.partial(scatter_kernel, n), out_shape=[jax.Shape...]
    all_gather x2 -> x0, waiting for transfers between devices: 196 us -> none  [the longest x1 102 us: body(): tok_all = lax.all_gather(tokens, 'ep', axis=0, tiled=False)]
    all_to_all x0 -> x2, starting transfers between devices: none -> 42.9 us  [the longest x1 35.6 us: body(): gg = lax.all_to_all(gg, 'ep', split_axis=0, concat_axis=0, tiled=True)]
    all_to_all x2 -> x0, blocking collectives: 24.1 us -> none  [the longest x1 14.3 us: body(): lax.all_to_all(weight, 'ep', split_axis=0, concat_axis=0, tiled=True)]
  transfers between devices with their start and end apart: 4 -> 2, of which waited for: 4 -> 0; matrix products, arithmetic and copies ran while one was open for 6% -> 12% of each run, Pallas kernels for 0% -> 63%
where the time goes in v2:
time: 474 us; the launch traced here: 473 us
  Pallas kernels  300 us (63%)
  matrix products  105 us (22%)
  starting transfers between devices  42.9 us (9%)
  other arithmetic  19.1 us (4%)
  local copies, waits for them, and re-layouts  4.91 us (1%)
    pallas_call x1, Pallas kernels, scatter_sums(): pl.pallas_call(functools.partial(scatter_kernel, n), out_shape=[jax.Shape...  154 us
    pallas_call x1, Pallas kernels, gather_blocks(): pl.pallas_call(functools.partial(gather_kernel, n), out_shape=[jax.ShapeD...  146 us
    all_to_all x1, starting transfers between devices, body(): gg = lax.all_to_all(gg, 'ep', split_axis=0, concat_axis=0, tiled=True)  35.6 us
    dot_general x2, matrix products, spread(): lax.dot_general(pick, rows.reshape(count, slots, width), (((1,), (1,)), (...  26.1 us
    dot_general x1, matrix products, body(): jnp.dot(hidden, wd, preferred_element_type=f32).astype(bf16).astype(f32)  15.9 us
    dot_general x2, matrix products, gather(): lax.dot_general(pick, x, (((2,), (1,)), ((0,), (0,))), preferred_element_...  15.2 us
    dot_general x1, matrix products, body(): lax.dot_general(ga, wg, (((1,), (1,)), ((), ())), preferred_element_type=...  14.7 us
    dot_general x1, matrix products, body(): lax.dot_general(gb, wu, (((1,), (1,)), ((), ())), preferred_element_type=...  11.5 us
  transfers between devices with their start and end apart: 2, of which 0 were waited for; matrix products, arithmetic and copies ran while one was open for 12% of the time, Pallas kernels for 63%

profile of v2, /device:TPU:0, one launch (start us, length us, event | category | flops | bytes accessed | tf_op | source)
XLA Modules:
  0.0 473.1 jit_solution(17413374023075625984)
XLA Ops:
  0.6 0.0 copy-start
  0.6 0.9 broadcast_in_dim.86
  1.5 0.1 reshape.60
  1.6 0.8 select_reduce_fusion.3
  2.5 0.7 add.23
  3.1 0.1 select_reduce_fusion.2
  3.2 1.4 fusion.21
  4.7 7.3 %all-to-all-start = ((f32[32,1,128]{2,1,0:T(1,128)}), f32[32,1,128]{2,1,0:T(1,128)S(1)}, u32[]{:S(2)}, u32[]{:S(2)}) async-start(f32[32,1,128]{2,1,0:T(1,128)} %bitcast.1), calls=%async_computation | async-start | bytes 32768 | tf_op jit(solution)/shard_map/all_to_all | solution.py:294
  12.0 146.3 %shard_map.112 = (bf16[32,128,2048]{2,1,0:T(8,128)(2,1)}, bf16[32,128,2048]{2,1,0:T(8,128)(2,1)}) custom-call(bf16[128,2048]{1,0:T(8,128)(2,1)} %refs_0_.1, bf16[128,2048]{1,0:T(8,128)(2,1)} %refs_1_.1), custom_call_target="tpu_custom_call" | custom-call | bytes 33554432 | tf_op jit(solution)/shard_map/pallas_call | solution.py:122
  158.3 0.1 fusion.15
  158.4 8.2 %convolution_convert_fusion.3 = bf16[32,48,2048]{2,1,0:T(8,128)(2,1)S(1)} fusion(bf16[32,128,2048]{2,1,0:T(8,128)(2,1)} %get-tuple-element.7, s32[32,128]{1,0:T(8,128)S(1)} %fusion.15), kind=kOutput, calls=%fused_computation.14 | convolution fusion | flops 808648704 | bytes 23085056 | tf_op jit(solution)/shard_map/dot_general | solution.py:305
  166.7 0.0 copy-start.5
  166.7 6.6 %fusion.10 = f32[1536,768]{1,0:T(8,128)} fusion(bf16[1536,2048]{1,0:T(8,128)(2,1)S(1)} %bitcast.37, bf16[1,2048,768]{2,1,0:T(8,128)(2,1)S(1)} %copy-done.4), kind=kOutput, calls=%fused_computation.23 | convolution fusion | flops 4831838208 | bytes 14155776 | tf_op jit(solution)/shard_map/dot_general | solution.py:316
  173.3 6.7 %fusion.6 = f32[1536,768]{1,0:T(8,128)} fusion(bf16[1536,2048]{1,0:T(8,128)(2,1)S(1)} %bitcast.38, bf16[1,2048,768]{2,1,0:T(8,128)(2,1)S(1)} %copy-done.5), kind=kOutput, calls=%fused_computation.19 | convolution fusion | flops 4831838208 | bytes 14155776 | tf_op jit(solution)/shard_map/dot_general | solution.py:317
  180.0 7.0 %convert_convert_fusion = f32[32,48,2048]{2,1,0:T(8,128)S(1)} fusion(bf16[32,128,2048]{2,1,0:T(8,128)(2,1)} %get-tuple-element.8, s32[32,128]{1,0:T(8,128)S(1)} %fusion.15), kind=kOutput, calls=%fused_computation.9 | convolution fusion | flops 811794432 | bytes 29376512 | tf_op jit(solution)/shard_map/dot_general | solution.py:305
  187.0 15.9 %fusion.1 = (f32[1536]{0:T(1024)S(1)}, bf16[1536,2048]{1,0:T(8,128)(2,1)}) fusion(f32[32,48,2048]{2,1,0:T(8,128)S(1)} %convert_convert_fusion, bf16[1,768,2048]{2,1,0:T(8,128)(2,1)S(1)} %copy-done, f32[1536,768]{1,0:T(8,128)} %fusion.6, f32[1536,768]{1,0:T(8,128)} %fusion.10), kind=kOutput, calls=%fused_computation.5 | convolution fusion | flops 4851497472 | bytes 31463424 | tf_op jit(solution)/shard_map/dot_general | solution.py:320
  203.0 0.1 broadcast_in_dim.94
  203.0 1.0 select_reduce_fusion
  204.0 8.0 %multiply_convert_fusion = bf16[32,48,2048]{2,1,0:T(8,128)(2,1)} fusion(f32[32,48,2048]{2,1,0:T(8,128)} %copy-done.2, f32[32,48]{1,0:T(8,128)S(1)} %get-tuple-element.12), kind=kLoop, calls=%fused_computation.7 | loop fusion | flops 6291456 | bytes 18880512 | tf_op jit(solution)/shard_map/convert_element_type | solution.py:327
  212.0 0.1 mul.63
  212.0 8.6 %fusion.2 = f32[1536,768]{1,0:T(8,128)} fusion(bf16[1536,2048]{1,0:T(8,128)(2,1)} %bitcast.39, bf16[1,768,2048]{2,1,0:T(8,128)(2,1)S(1)} %copy-done), kind=kOutput, calls=%fused_computation.15 | convolution fusion | flops 4831838208 | bytes 14155776 | tf_op jit(solution)/shard_map/dot_general | solution.py:328
  220.7 35.6 %all-to-all-start.1 = ((f32[32,1,128]{2,1,0:T(1,128)}), f32[32,1,128]{2,1,0:T(1,128)S(1)}, u32[]{:S(2)}, u32[]{:S(2)}) async-start(f32[32,1,128]{2,1,0:T(1,128)} %bitcast.11), calls=%async_computation.1 | async-start | bytes 32768 | tf_op jit(solution)/shard_map/all_to_all | solution.py:325
  256.2 0.0 copy-start.6
  256.3 14.7 %fusion.8 = f32[1536,2048]{1,0:T(8,128)} fusion(bf16[1,2048,768]{2,1,0:T(8,128)(2,1)} %param.15, f32[1536,768]{1,0:T(8,128)} %fusion.10, f32[1536,768]{1,0:T(8,128)} %fusion.2, f32[1536,768]{1,0:T(8,128)} %fusion.6), kind=kOutput, calls=%fused_computation.21 | convolution fusion | flops 4843634688 | bytes 29884416 | tf_op jit(solution)/shard_map/dot_general | solution.py:331
  271.0 11.5 %add_convert_fusion = bf16[1536,2048]{1,0:T(8,128)(2,1)} fusion(f32[1536,2048]{1,0:T(8,128)} %fusion.8, bf16[1,2048,768]{2,1,0:T(8,128)(2,1)S(1)} %copy-done.6, f32[1536,768]{1,0:T(8,128)S(1)} %copy-done.7, f32[1536,768]{1,0:T(8,128)} %fusion.10), kind=kOutput, calls=%fused_computation.6 | convolution fusion | flops 4845207552 | bytes 31457280 | tf_op jit(solution)/shard_map/dot_general | solution.py:332
  282.4 13.0 %convolution_convert_fusion.refs_1_ = bf16[32,128,2048]{2,1,0:T(8,128)(2,1)} fusion(bf16[32,48,2048]{2,1,0:T(8,128)(2,1)} %bitcast.40, s32[32,128]{1,0:T(8,128)S(1)} %fusion.15), kind=kOutput, calls=%fused_computation.2 | convolution fusion | flops 813891584 | bytes 23085056 | tf_op jit(solution)/shard_map/dot_general | solution.py:310
  295.5 6.5 %fusion = bf16[1536,2048]{1,0:T(8,128)(2,1)} fusion(bf16[1536,2048]{1,0:T(8,128)(2,1)} %get-tuple-element.14, f32[1536]{0:T(1024)S(1)} %mul.63), kind=kLoop, calls=%fused_computation.4 | loop fusion | flops 9437184 | bytes 12589056 | tf_op jit(solution)/shard_map/convert_element_type | solution.py:321
  301.9 13.0 %convolution_convert_fusion.1.refs_0_ = bf16[32,128,2048]{2,1,0:T(8,128)(2,1)} fusion(bf16[32,48,2048]{2,1,0:T(8,128)(2,1)} %bitcast.36, s32[32,128]{1,0:T(8,128)S(1)} %fusion.15), kind=kOutput, calls=%fused_computation.3 | convolution fusion | flops 813891584 | bytes 23085056 | tf_op jit(solution)/shard_map/dot_general | solution.py:310
  315.0 153.7 %shard_map.113 = (bf16[128,2048]{1,0:T(8,128)(2,1)}, bf16[128,2048]{1,0:T(8,128)(2,1)}) custom-call(bf16[32,128,2048]{2,1,0:T(8,128)(2,1)} %convolution_convert_fusion.1.refs_0_, bf16[32,128,2048]{2,1,0:T(8,128)(2,1)} %convolution_convert_fusion.refs_1_), custom_call_target="tpu_custom_call" | custom-call | bytes 33554432 | tf_op jit(solution)/shard_map/pallas_call | solution.py:251
  468.7 0.7 fusion.22
  469.4 1.9 copy.21
  471.2 1.9 copy.22
  (16 shorter events, 0.0 us)
Async XLA Ops:
  0.6 186.4 %copy-start = (bf16[1,768,2048]{2,1,0:T(8,128)(2,1)S(1)}, bf16[1,768,2048]{2,1,0:T(8,128)(2,1)}, u32[]{:S(2)}) copy-start(bf16[1,768,2048]{2,1,0:T(8,128)(2,1)} %param.17) | copy-start | bytes 9437188
  4.7 153.6 %all-to-all-start = ((f32[32,1,128]{2,1,0:T(1,128)}), f32[32,1,128]{2,1,0:T(1,128)S(1)}, u32[]{:S(2)}, u32[]{:S(2)}) async-start(f32[32,1,128]{2,1,0:T(1,128)} %bitcast.1), calls=%async_computation | async-start | bytes 32768 | tf_op jit(solution)/shard_map/all_to_all | solution.py:294
  158.4 8.2 %copy-start.4 = (bf16[1,2048,768]{2,1,0:T(8,128)(2,1)S(1)}, bf16[1,2048,768]{2,1,0:T(8,128)(2,1)}, u32[]{:S(2)}) copy-start(bf16[1,2048,768]{2,1,0:T(8,128)(2,1)} %param.15) | copy-start | bytes 9437188
  166.7 6.6 %copy-start.5 = (bf16[1,2048,768]{2,1,0:T(8,128)(2,1)S(1)}, bf16[1,2048,768]{2,1,0:T(8,128)(2,1)}, u32[]{:S(2)}) copy-start(bf16[1,2048,768]{2,1,0:T(8,128)(2,1)} %param.16) | copy-start | bytes 9437188
  187.0 16.0 %copy-start.2 = (f32[32,48,2048]{2,1,0:T(8,128)}, f32[32,48,2048]{2,1,0:T(8,128)S(1)}, u32[]{:S(2)}) copy-start(f32[32,48,2048]{2,1,0:T(8,128)S(1)} %convert_convert_fusion) | copy-start | bytes 37748740
  220.7 248.0 %all-to-all-start.1 = ((f32[32,1,128]{2,1,0:T(1,128)}), f32[32,1,128]{2,1,0:T(1,128)S(1)}, u32[]{:S(2)}, u32[]{:S(2)}) async-start(f32[32,1,128]{2,1,0:T(1,128)} %bitcast.11), calls=%async_computation.1 | async-start | bytes 32768 | tf_op jit(solution)/shard_map/all_to_all | solution.py:325
  256.2 14.7 %copy-start.6 = (bf16[1,2048,768]{2,1,0:T(8,128)(2,1)S(1)}, bf16[1,2048,768]{2,1,0:T(8,128)(2,1)}, u32[]{:S(2)}) copy-start(bf16[1,2048,768]{2,1,0:T(8,128)(2,1)} %param.16) | copy-start | bytes 9437188
  256.2 14.7 %copy-start.7 = (f32[1536,768]{1,0:T(8,128)S(1)}, f32[1536,768]{1,0:T(8,128)}, u32[]{:S(2)}) copy-start(f32[1536,768]{1,0:T(8,128)} %fusion.2) | copy-start | bytes 14155780
  315.0 153.7 %copy-start.3 = (s32[128,8]{0,1:T(8,128)S(1)}, s32[128,8]{0,1:T(8,128)}, u32[]{:S(2)}) copy-start(s32[128,8]{0,1:T(8,128)} %param.12) | copy-start | bytes 12292
  315.0 158.2 %copy-start.1 = (bf16[1,768,2048]{2,1,0:T(8,128)(2,1)S(1)}, bf16[1,768,2048]{2,1,0:T(8,128)(2,1)}, u32[]{:S(2)}) copy-start(bf16[1,768,2048]{2,1,0:T(8,128)(2,1)} %param.17) | copy-start | bytes 9437188
